TPU v7x, 512 devices: a whole 4x8x8 slice. The times are simulated.
512 devices in a mesh: ctx: 64 (over z, y), node: 8 (over x, core).
Axes of the slice: x: 4, y: 8, z: 8, core: 2. Of those that a mesh axis runs over, the one named last changes fastest.
Arguments:
- tokens: bfloat16 [131072, 512], P(('ctx', 'node')), may hold values from -64 to 64
- w_query: bfloat16 [512, 512], replicated, may hold values from -0.25 to 0.25
- w_key: bfloat16 [512, 512], replicated, may hold values from -0.25 to 0.25
- w_value: bfloat16 [512, 512], replicated, may hold values from -0.25 to 0.25
- w_out: bfloat16 [512, 512], replicated, may hold values from -0.25 to 0.25
Outputs:
- mixed: bfloat16 [131072, 512], P(('ctx', 'node'))
All inputs are finite; a program needn't handle non-finite values.
Results may differ from a plain program's by a relative error of at most 0.012.
Values may be sent and summed in bfloat16 or wider, within the bound.
A program may use at most 64 MiB of HBM per device.

v0:
```python
import functools
import math

import jax
import jax.numpy as jnp
from jax import lax
from jax.experimental import pallas as pl
from jax.experimental.pallas import tpu as pltpu
from jax.sharding import PartitionSpec as P

HEADS = 8
HEAD = 64
WIDTH = HEADS * HEAD
BLOCK = 128
ROWS = 256
NODES = 8
FAR = 1e30
SCALE = math.log2(math.e) / math.sqrt(HEAD)
BF16 = jnp.bfloat16
F32 = jnp.float32
START = {1: 0, 2: 128, 3: 192, 4: 224}
COARSE = 240


def nn(a, b):
    return lax.dot_general(a, b, (((1,), (0,)), ((), ())), preferred_element_type=F32)


def nt(a, b):
    return lax.dot_general(a, b, (((1,), (1,)), ((), ())), preferred_element_type=F32)


def iota(shape, axis):
    return lax.broadcasted_iota(jnp.int32, shape, axis)


def averager(rows, columns, level):
    hit = iota((rows, columns), 0) == iota((rows, columns), 1) >> level
    return jnp.where(hit, 0.5**level, 0.0).astype(BF16)


def spreader(rows, queries, level):
    hit = (iota((rows, ROWS), 0) & (queries - 1)) == iota((rows, ROWS), 1) >> level
    return jnp.where(hit, 1.0, 0.0).astype(BF16)


def split(values):
    high = values.astype(BF16)
    rest = values - high.astype(F32)
    middle = rest.astype(BF16)
    return [high, middle, (rest - middle.astype(F32)).astype(BF16)]


def spread_all(sums, tops, totals, spread):
    rows = sums.shape[0]
    out = nn(jnp.concatenate([sums] + split(jnp.concatenate([tops, totals], 0)), 0), spread)
    stats = out[rows : rows + 16] + out[rows + 16 : rows + 32] + out[rows + 32 :]
    return out[:rows], stats[:8], stats[8:]


def lane_head(shape, width):
    return iota(shape, 1) >> (width.bit_length() - 1)


def kernel(
    devices, x_hbm, wq_hbm, wk_hbm, wv_hbm, wo_hbm, out_ref,
    x, wq, wk, wv, wo, wvt, t, hnear, hfar, deep, q0, ql, k0, v0, kh, vh, u2, u3, u4, vd, acc, peak, den,
    average, eye, halve, fold, spread1, spread2, spread3, spread4,
    load_sem, send_sem, recv01, recv_far, recv_near,
):
    me = lax.axis_index("ctx") * NODES + lax.axis_index("node")
    core = lax.rem(me, 2)
    chip = lax.div(me, 2)
    pair = lax.div(me, 4)
    group = lax.div(me, 8)

    def place(index):
        return {"ctx": lax.div(index, NODES), "node": lax.rem(index, NODES)}

    def exists(index):
        return jnp.logical_and(index >= 0, index < devices)

    loads = []
    for i, (source, kept) in enumerate(((x_hbm, x), (wq_hbm, wq), (wk_hbm, wk), (wv_hbm, wv), (wo_hbm, wo))):
        loads.append(pltpu.make_async_copy(source, kept, load_sem.at[i]))
    loads[0].start()

    twin = me + 1 - 2 * core
    beyond = me - 1 + 2 * core
    odd = lax.rem(chip, 2)
    second = lax.rem(pair, 2)
    two = me + 3 - 6 * core
    three_ahead = [(me + 4 - 8 * odd, odd, 1), (me + 6 - 12 * odd, odd, 0)]
    three_behind = [(me - 4 + 8 * odd, 1 - odd, 0)]
    ahead = 8 * (group + 1 - 2 * second) + core
    behind = 8 * (group - 1 + 2 * second) + core
    four_ahead = [(ahead + 4 * second + 2 * j, second, 1) for j in range(2)]
    four_ahead += [(ahead + 4 * (1 - second) + 2 * j, second, 0) for j in range(2)]
    four_behind = [(behind + 4 * second + 2 * j, 1 - second, 0) for j in range(2)]
    there = [exists(beyond), exists(two), exists(three_ahead[0][0]), exists(three_behind[0][0])]
    there += [exists(ahead), exists(behind)]
    parties = [[beyond], [two]] + [[p[0] for p in ps] for ps in (three_ahead, three_behind, four_ahead, four_behind)]

    barrier = pltpu.get_barrier_semaphore()

    def signal(target):
        pl.semaphore_signal(barrier, inc=1, device_id=place(target), device_id_type=pl.DeviceIdType.MESH)

    expected = 1
    for here, targets in zip(there, parties):
        expected = expected + jnp.where(here, len(targets), 0)
        pl.when(here)(lambda targets=targets: [signal(target) for target in targets] and None)
    signal(twin)
    for load in loads[1:]:
        load.start()

    pl.semaphore_wait(barrier, expected)

    def send(source, target, landing, recv, sent):
        pltpu.make_async_remote_copy(
            src_ref=source,
            dst_ref=landing,
            send_sem=send_sem.at[sent],
            recv_sem=recv,
            device_id=place(target),
            device_id_type=pl.DeviceIdType.MESH,
        ).start()

    def mine(direction):
        return core * BLOCK + direction * 64

    def send_edge(target, half, landing, recv, sent):
        rows = pl.multiple_of(half * BLOCK, BLOCK)
        send(x_hbm.at[pl.ds(rows, BLOCK)], target, landing.at[pl.ds(0, BLOCK)], recv, sent)

    pl.when(there[0])(lambda: send_edge(beyond, core, hfar, recv01.at[1], 1))
    send_edge(twin, 1 - core, hnear, recv01.at[0], 0)

    h2, h3, h4 = (deep.at[pl.ds(i * ROWS, ROWS)] for i in range(3))
    for l in range(1, 5):
        average[START[l] : START[l] + (ROWS >> l), :] = averager(ROWS >> l, ROWS, l)
    loads[0].wait()
    t[...] = nn(average[...], x[...]).astype(BF16)

    def send_one_means(target, half, landing, recv, sent):
        means = pl.multiple_of((1 - half) * 64, 64)
        send(t.at[pl.ds(means, 64)], target, landing.at[pl.ds(BLOCK, 64)], recv, sent)

    @pl.when(there[0])
    def _():
        send_one_means(beyond, core, hfar, recv01.at[1], 1)

    @pl.when(there[1])
    def _():
        landing = h2.at[pl.ds(pl.multiple_of(BLOCK - core * 64, 64), 64)]
        send(t.at[pl.ds(START[2], 64)], two, landing, recv_far.at[0], 2)

    def send_three(targets, sent):
        for target, d, short in targets:
            landing = h3.at[pl.ds(pl.multiple_of(mine(d) + odd * 32, 32), 32)]
            send(t.at[pl.ds(START[3], 32)], target, landing, recv_far.at[2 + short], sent)

    def send_four(targets, sent):
        for target, d, short in targets:
            landing = h4.at[pl.ds(pl.multiple_of(mine(d) + lax.rem(chip, 4) * 16, 16), 16)]
            send(t.at[pl.ds(START[4], 16)], target, landing, recv_far.at[4 + short], sent)

    pl.when(there[2])(lambda: send_three(three_ahead, 3))
    pl.when(there[3])(lambda: send_three(three_behind, 4))
    pl.when(there[4])(lambda: send_four(four_ahead, 5))
    pl.when(there[5])(lambda: send_four(four_behind, 6))
    send_one_means(twin, 1 - core, hnear, recv01.at[0], 0)

    def landed(buffer, start, rows, sem):
        region = buffer.at[pl.ds(start, rows)]
        pltpu.make_async_copy(region, region, sem).wait()

    def landed_or_zero(here, buffer, start, rows, sem):
        pl.when(here)(lambda: landed(buffer, start, rows, sem))

        @pl.when(jnp.logical_not(here))
        def _():
            buffer[pl.ds(start, rows), :] = jnp.zeros((rows, WIDTH), BF16)

    def half_of(buffer, whose):
        return buffer.at[pl.ds(pl.multiple_of(whose * BLOCK, BLOCK), BLOCK)]

    def forward(buffer, which):
        region = half_of(buffer, core)
        send(region, twin, region, recv_near.at[which], 0)

    def finer(source, d, target, inside):
        rows = source[pl.ds(pl.multiple_of(mine(d), 64), 64), :]
        means = nn(halve[:32, :64], rows).astype(BF16)
        target[pl.ds(pl.multiple_of(mine(d) + inside * 32, 32), 32), :] = means

    ones = jnp.ones((16, ROWS), BF16)
    half = lane_head((1, BLOCK), HEAD)
    pair_masks = [jnp.where(half == h, 1.0, 0.0).astype(BF16) for h in range(2)]

    def lanes_of(j):
        return slice(j * BLOCK, (j + 1) * BLOCK)

    def head_rows(h):
        return slice(h * HEAD, (h + 1) * HEAD)

    def pair_queries(block):
        return jnp.concatenate([block * pair_masks[0], block * pair_masks[1]], 0)

    def with_ones(v):
        return jnp.concatenate([v, ones[:, : v.shape[1]]], 0)

    def merge(lanes, top, total, heads):
        before = peak[:, lanes]
        after = jnp.maximum(before, top)
        old = jnp.exp2(before - after)
        new = jnp.exp2(top - after)
        den[:, lanes] = den[:, lanes] * old + new * total
        peak[:, lanes] = after
        for h in range(HEADS):
            rows = head_rows(h)
            acc[rows, lanes] = acc[rows, lanes] * old[h : h + 1] + heads(h) * new[h : h + 1]

    def run(units):
        waiting, active = list(units), []
        while waiting or active:
            if waiting:
                active.append(waiting.pop(0))
            active = [unit for unit in active if next(unit, None) is not None]

    def attend(keys, queries, values, done):
        s = nt(keys(), queries())
        yield True
        m = jnp.max(s, axis=0, keepdims=True)
        p = jnp.exp2(s - m).astype(BF16)
        yield True
        done(m, nn(with_ones(values()), p))

    def base_own(h):
        pairs = lanes_of(h // 2)

        def done(m, o):
            peak[h : h + 1, :] = m
            den[h : h + 1, :] = o[HEAD : HEAD + 1]
            acc[head_rows(h), :] = o[:HEAD]

        return attend(
            lambda: k0[:, pairs], lambda: q0[:, pairs] * pair_masks[h % 2], lambda: v0[head_rows(h), :], done
        )

    def project_side(buffer, slot):
        rows = buffer[...]
        kh[slot, :192, :] = nn(rows, wk[...]).astype(BF16)
        vh[slot, :, :192] = nt(wvt[...], rows).astype(BF16)

    def halve_side(slot):
        kh[slot, 192:, :] = nn(halve[...], kh[slot, :BLOCK, :]).astype(BF16)
        vh[slot, :, 192:] = nt(vh[slot, :, :BLOCK], halve[...]).astype(BF16)

    def side(slot, block):
        queries = pl.ds(pl.multiple_of(block * BLOCK, BLOCK), BLOCK)
        units, found = [], ([], [])
        for keys, q, part in (
            (slice(0, BLOCK), q0.at[queries], found[0]),
            (slice(BLOCK, 2 * BLOCK), ql.at[pl.ds(0, BLOCK)], found[1]),
        ):
            for j in range(HEADS // 2):
                units.append(
                    attend(
                        lambda keys=keys, j=j: kh[slot, keys, lanes_of(j)],
                        lambda q=q, j=j: pair_queries(q[:, lanes_of(j)]),
                        lambda keys=keys, j=j: vh[slot, lanes_of(j), keys],
                        lambda m, o, part=part: part.append((m, o)),
                    )
                )
        return units, queries, found[0], found[1]

    def by_head(part):
        tops = [m[:, lanes_of(h)] for m, _ in part for h in range(2)]
        totals = [o[BLOCK : BLOCK + 1, lanes_of(h)] for _, o in part for h in range(2)]
        sums = [o[head_rows(h), lanes_of(h)] for _, o in part for h in range(2)]
        return jnp.concatenate(tops, 0), jnp.concatenate(totals, 0), sums

    def off(missing):
        return jnp.where(missing, FAR, 0.0).astype(F32)

    everywhere = slice(0, ROWS)

    seen = {2: u2, 3: u3, 4: u4}

    def shape_of(level):
        queries = ROWS >> level
        together = min(HEADS, ROWS // queries)
        return queries, together, together * queries

    def look(level):
        queries = ROWS >> level
        for u in range(2):
            part = slice(u * ROWS, (u + 1) * ROWS)
            block = ql[START[level] : START[level] + queries, part]
            masked = [block * jnp.where(lane_head((1, ROWS), HEAD) == h, 1.0, 0.0).astype(BF16) for h in range(4)]
            rows = slice(u * 4 * queries, (u + 1) * 4 * queries)
            seen[level][rows, :] = nt(jnp.concatenate(masked, 0), wk[:, part]).astype(BF16)

    def rows_of(level, whose):
        return half_of((h2, h3, h4)[level - 2], whose)[...]

    def values_of(whose):
        return nt(wvt[...], jnp.concatenate([rows_of(l, whose) for l in range(2, 5)], 0)).astype(BF16)

    scores = {}

    def coarse(level, index, count):
        queries, together, columns = shape_of(level)
        features = together * HEAD
        lanes = lanes_of(level - 2)
        off_left, off_right = off(index == 0), off(index == count - 1)
        column_head = lane_head((1, columns), queries)
        found = []

        def unit(u):
            part = slice(u * features, (u + 1) * features)
            s = [scores[level, u], nt(rows_of(level, 1 - core), seen[level][u * columns : (u + 1) * columns, :])]
            yield True
            left = [half[:64] for half in s]
            right = [half[64:] for half in s]
            m = jnp.maximum(
                jnp.max(jnp.maximum(*left), axis=0, keepdims=True) - off_left,
                jnp.max(jnp.maximum(*right), axis=0, keepdims=True) - off_right,
            )
            p = []
            for half in range(2):
                p.append(jnp.exp2(left[half] - (m + off_left)).astype(BF16))
                p.append(jnp.exp2(right[half] - (m + off_right)).astype(BF16))
            yield True
            values = jnp.concatenate([vd[0, part, lanes], vd[1, part, lanes]], 1)
            o = nn(with_ones(values), jnp.concatenate(p, 0))
            yield True
            own = [jnp.where(column_head == h, o[head_rows(h)], 0.0) for h in range(together)]
            row_head = iota((HEADS, columns), 0) == column_head + u * together
            found.append(
                spread_all(
                    jnp.concatenate(own, 0).astype(BF16),
                    jnp.where(row_head, m, 0.0),
                    jnp.where(row_head, o[features : features + 1], 0.0),
                    spreads[level][...],
                )
            )

        def gathered():
            def heads(h):
                u, inside = divmod(h, together)
                return found[u][0][head_rows(inside)]

            top = functools.reduce(jnp.add, [f[1] for f in found])
            total = functools.reduce(jnp.add, [f[2] for f in found])
            return top, total, heads, 2.0**level

        return [unit(u) for u in range(HEADS // together)], gathered

    eye[...] = averager(ROWS, ROWS, 0)
    halve[...] = averager(64, BLOCK, 1)
    fold[:32, :] = jnp.concatenate([averager(32, BLOCK, 2), jnp.zeros((32, 64), BF16)], 1)
    fold[32:, :] = jnp.concatenate([jnp.zeros((32, BLOCK), BF16), averager(32, 64, 1)], 1)
    spreads = {1: spread1, 2: spread2, 3: spread3, 4: spread4}
    for l in range(1, 5):
        spreads[l][...] = spreader(spreads[l].shape[0], ROWS >> l, l)
    for load in loads[1:4]:
        load.wait()
    q0[...] = (nn(x[...], wq[...]) * SCALE).astype(BF16)
    k0[...] = nn(x[...], wk[...]).astype(BF16)
    for i in range(2):
        wvt[i * ROWS : (i + 1) * ROWS, :] = nt(eye[...], wv[:, i * ROWS : (i + 1) * ROWS]).astype(BF16)
    ql[...] = nn(average[...], q0[...]).astype(BF16)
    v0[...] = nt(wvt[...], x[...]).astype(BF16)

    landed(hnear, 0, 192, recv01.at[0])
    project_side(hnear, 0)
    units, near_lanes, base_near, one_near = side(0, 1 - core)
    own_units = [base_own(h) for h in range(HEADS)]
    run(own_units[:4])
    halve_side(0)
    run(own_units[4:] + units)
    top, total, near_sums = by_head(base_near)
    merge(near_lanes, top, total, lambda h: near_sums[h])
    for l in range(2, 5):
        look(l)

    landed_or_zero(there[0], hfar, 0, 192, recv01.at[1])
    h2[pl.ds(pl.multiple_of(mine(core), 64), 64), :] = nn(fold[...], hfar[...]).astype(BF16)
    landed_or_zero(there[1], h2, pl.multiple_of(mine(1 - core), 64), 64, recv_far.at[0])
    forward(h2, 0)
    finer(h2, odd, h3, 1 - odd)
    project_side(hfar, 1)
    landed_or_zero(there[2], h3, pl.multiple_of(mine(1 - odd), 64), 64, recv_far.at[2])
    landed_or_zero(there[3], h3, pl.multiple_of(mine(odd) + odd * 32, 32), 32, recv_far.at[3])
    forward(h3, 1)
    finer(h3, second, h4, 1 - second)
    halve_side(1)
    landed_or_zero(there[4], h4, pl.multiple_of(mine(1 - second), 64), 64, recv_far.at[4])
    landed_or_zero(there[5], h4, pl.multiple_of(mine(second) + second * 32, 32), 32, recv_far.at[5])
    forward(h4, 2)

    units, far_lanes, base_far, one_far = side(1, core)
    run(units)
    missing = off(jnp.where(core == 0, me == 0, me == devices - 1))
    top, total, far_sums = by_head(base_far)
    merge(far_lanes, top - missing, total, lambda h: far_sums[h])
    near_top, near_total, near_one = by_head(one_near)
    far_top, far_total, far_one = by_head(one_far)
    far_top = far_top - missing
    top = jnp.maximum(near_top, far_top)
    factor_near = jnp.exp2(near_top - top)
    factor_far = jnp.exp2(far_top - top)
    total = near_total * factor_near + far_total * factor_far
    sums = [
        (near_one[h] * factor_near[h : h + 1] + far_one[h] * factor_far[h : h + 1]).astype(BF16)
        for h in range(HEADS)
    ]
    one_sums, top, total = spread_all(jnp.concatenate(sums, 0), top, total, spread1[...])
    terms = [(top, total, lambda h: one_sums[head_rows(h)], 2.0)]

    vd[0] = values_of(core)
    for l in range(4, 1, -1):
        _, together, columns = shape_of(l)
        for u in range(HEADS // together):
            scores[l, u] = nt(rows_of(l, core), seen[l][u * columns : (u + 1) * columns, :])
    for i, buffer in enumerate((h2, h3, h4)):
        landed(buffer, pl.multiple_of((1 - core) * BLOCK, BLOCK), BLOCK, recv_near.at[i])
    vd[1] = values_of(1 - core)
    levels = [coarse(4, group, devices // 8), coarse(3, pair, devices // 4), coarse(2, chip, devices // 2)]
    run([unit for units, _ in levels for unit in units])
    terms += [gathered() for _, gathered in levels]

    before = peak[...]
    after = functools.reduce(jnp.maximum, [term[0] for term in terms], before)
    factors = [jnp.exp2(before - after)] + [weight * jnp.exp2(top - after) for top, _, _, weight in terms]
    lower = den[...] * factors[0]
    for factor, term in zip(factors[1:], terms):
        lower = lower + factor * term[1]
    factors = [factor / lower for factor in factors]
    attended = []
    for h in range(HEADS):
        upper = acc[head_rows(h), :] * factors[0][h : h + 1]
        for factor, term in zip(factors[1:], terms):
            upper = upper + term[2](h) * factor[h : h + 1]
        attended.append(upper.astype(BF16))
    loads[4].wait()
    turned = nt(eye[...], jnp.concatenate(attended, 0)).astype(BF16)
    out_ref[...] = nn(turned, wo[...]).astype(BF16)

    landed(deep, 0, 192 + 3 * BLOCK, send_sem.at[0])
    for i, (here, rows) in enumerate(zip(there, (192, 64, 64, 32, 64, 32))):
        pl.when(here)(lambda i=i, rows=rows: landed(deep, 0, rows, send_sem.at[i + 1]))


def solution(mesh):
    devices = mesh.shape["ctx"] * mesh.shape["node"]

    def local(tokens, w_query, w_key, w_value, w_out):
        square = pltpu.VMEM((WIDTH, WIDTH), BF16)
        tall = pltpu.VMEM((ROWS, WIDTH), BF16)
        return pl.pallas_call(
            functools.partial(kernel, devices),
            out_shape=jax.ShapeDtypeStruct((ROWS, WIDTH), BF16),
            in_specs=[pl.BlockSpec(memory_space=pltpu.HBM)] * 5,
            out_specs=pl.BlockSpec(memory_space=pltpu.VMEM),
            scratch_shapes=[
                tall,
                square,
                square,
                square,
                square,
                square,
                pltpu.VMEM((COARSE, WIDTH), BF16),
                pltpu.VMEM((192, WIDTH), BF16),
                pltpu.VMEM((192, WIDTH), BF16),
                pltpu.VMEM((3 * ROWS, WIDTH), BF16),
                tall,
                pltpu.VMEM((COARSE, WIDTH), BF16),
                tall,
                pltpu.VMEM((WIDTH, ROWS), BF16),
                pltpu.VMEM((2, ROWS, WIDTH), BF16),
                pltpu.VMEM((2, WIDTH, ROWS), BF16),
                square,
                tall,
                pltpu.VMEM((BLOCK, WIDTH), BF16),
                pltpu.VMEM((2, WIDTH, 3 * BLOCK), BF16),
                pltpu.VMEM((WIDTH, ROWS), F32),
                pltpu.VMEM((HEADS, ROWS), F32),
                pltpu.VMEM((HEADS, ROWS), F32),
                pltpu.VMEM((COARSE, ROWS), BF16),
                pltpu.VMEM((ROWS, ROWS), BF16),
                pltpu.VMEM((64, BLOCK), BF16),
                pltpu.VMEM((64, 192), BF16),
                pltpu.VMEM((BLOCK, ROWS), BF16),
                pltpu.VMEM((ROWS, ROWS), BF16),
                pltpu.VMEM((ROWS, ROWS), BF16),
                pltpu.VMEM((BLOCK, ROWS), BF16),
                pltpu.SemaphoreType.DMA((5,)),
                pltpu.SemaphoreType.DMA((7,)),
                pltpu.SemaphoreType.DMA((2,)),
                pltpu.SemaphoreType.DMA((6,)),
                pltpu.SemaphoreType.DMA((3,)),
            ],
            compiler_params=pltpu.CompilerParams(
                collective_id=0, has_side_effects=True, vmem_limit_bytes=40 * 2**20
            ),
            name="hierarchical_attention",
        )(*[pltpu.with_memory_space_constraint(a, pltpu.HBM) for a in (tokens, w_query, w_key, w_value, w_out)])

    placed = (P(("ctx", "node"), None), P(), P(), P(), P())
    return jax.shard_map(
        local, mesh=mesh, in_specs=placed, out_specs=P(("ctx", "node"), None), check_vma=False
    )
```

profile of v0, /device:TPU:256, one launch (start us, length us, event | category | flops | bytes accessed | tf_op | source)
XLA Modules:
  0.0 19.6 jit_solution(6689798648812414938)
XLA Ops:
  0.0 18.9 %hierarchical_attention.1 = bf16[256,512]{1,0:T(8,128)(2,1)S(1)} custom-call(bf16[256,512]{1,0:T(8,128)(2,1)} %x_hbm.1, bf16[512,512]{1,0:T(8,128)(2,1)} %wq_hbm.1, bf16[512,512]{1,0:T(8,128)(2,1)} %wk_hbm.1, bf16[512,512]{1,0:T(8,128)(2,1)} %wv_hbm.1, bf16[512,512]{1,0:T(8,128)(2,1)} %wo_hbm.1), custom_call_target="tpu_custom_call" | custom-call | tf_op jit(solution)/shard_map/hierarchical_attention/pallas_call | solution.py:463
  18.9 0.7 %copy.7 = bf16[256,512]{1,0:T(8,128)(2,1)} copy(bf16[256,512]{1,0:T(8,128)(2,1)S(1)} %hierarchical_attention.1) | data formatting | bytes 524288
where the time goes:
time: 19.8 us; the launch traced here: 19.6 us
  Pallas kernels  18.9 us (95%)
  local copies, waits for them, and re-layouts  0.71 us (4%)
    pallas_call x1, Pallas kernels, local(): pl.pallas_call(functools.partial(kernel, devices), out_shape=jax.ShapeDty...  18.9 us
    unnamed x1, local copies, waits for them, and re-layouts  0.71 us

commit v1 on v0

--- a/solution.py
+++ b/solution.py
@@ -114,6 +114,12 @@
     for load in loads[1:]:
         load.start()
 
+    h2, h3, h4 = (deep.at[pl.ds(i * ROWS, ROWS)] for i in range(3))
+    for l in range(1, 5):
+        average[START[l] : START[l] + (ROWS >> l), :] = averager(ROWS >> l, ROWS, l)
+    loads[0].wait()
+    t[...] = nn(average[...], x[...]).astype(BF16)
+
     pl.semaphore_wait(barrier, expected)
 
     def send(source, target, landing, recv, sent):
@@ -135,12 +141,6 @@
 
     pl.when(there[0])(lambda: send_edge(beyond, core, hfar, recv01.at[1], 1))
     send_edge(twin, 1 - core, hnear, recv01.at[0], 0)
-
-    h2, h3, h4 = (deep.at[pl.ds(i * ROWS, ROWS)] for i in range(3))
-    for l in range(1, 5):
-        average[START[l] : START[l] + (ROWS >> l), :] = averager(ROWS >> l, ROWS, l)
-    loads[0].wait()
-    t[...] = nn(average[...], x[...]).astype(BF16)
 
     def send_one_means(target, half, landing, recv, sent):
         means = pl.multiple_of((1 - half) * 64, 64)
@@ -249,31 +249,34 @@
         )
 
     def project_side(buffer, slot):
-        rows = buffer[...]
-        kh[slot, :192, :] = nn(rows, wk[...]).astype(BF16)
-        vh[slot, :, :192] = nt(wvt[...], rows).astype(BF16)
-
-    def halve_side(slot):
-        kh[slot, 192:, :] = nn(halve[...], kh[slot, :BLOCK, :]).astype(BF16)
-        vh[slot, :, 192:] = nt(vh[slot, :, :BLOCK], halve[...]).astype(BF16)
+        buffer[192:, :] = nn(halve[...], buffer[:BLOCK, :]).astype(BF16)
+        kh[slot] = nn(buffer[...], wk[...]).astype(BF16)
+        vh[slot] = nt(wvt[...], buffer[...]).astype(BF16)
 
     def side(slot, block):
         queries = pl.ds(pl.multiple_of(block * BLOCK, BLOCK), BLOCK)
-        units, found = [], ([], [])
-        for keys, q, part in (
-            (slice(0, BLOCK), q0.at[queries], found[0]),
-            (slice(BLOCK, 2 * BLOCK), ql.at[pl.ds(0, BLOCK)], found[1]),
-        ):
-            for j in range(HEADS // 2):
-                units.append(
-                    attend(
-                        lambda keys=keys, j=j: kh[slot, keys, lanes_of(j)],
-                        lambda q=q, j=j: pair_queries(q[:, lanes_of(j)]),
-                        lambda keys=keys, j=j: vh[slot, lanes_of(j), keys],
-                        lambda m, o, part=part: part.append((m, o)),
-                    )
-                )
-        return units, queries, found[0], found[1]
+        found = []
+        units = [
+            attend(
+                lambda j=j: kh[slot, :BLOCK, lanes_of(j)],
+                lambda j=j: pair_queries(q0[queries, lanes_of(j)]),
+                lambda j=j: vh[slot, lanes_of(j), :BLOCK],
+                lambda m, o: found.append((m, o)),
+            )
+            for j in range(HEADS // 2)
+        ]
+        return units, queries, found
+
+    def level_one(j, missing, found):
+        queries = pair_queries(ql[:BLOCK, lanes_of(j)])
+        s = nt(kh[:, BLOCK:, lanes_of(j)].reshape(ROWS, BLOCK), queries)
+        yield True
+        near, far = s[:BLOCK], s[BLOCK:]
+        m = jnp.maximum(jnp.max(near, axis=0, keepdims=True), jnp.max(far, axis=0, keepdims=True) - missing)
+        p = jnp.concatenate([jnp.exp2(near - m).astype(BF16), jnp.exp2(far - (m + missing)).astype(BF16)], 0)
+        yield True
+        values = jnp.concatenate([vh[0, lanes_of(j), BLOCK:], vh[1, lanes_of(j), BLOCK:]], 1)
+        found.append((m, nn(with_ones(values), p)))
 
     def by_head(part):
         tops = [m[:, lanes_of(h)] for m, _ in part for h in range(2)]
@@ -301,6 +304,7 @@
             masked = [block * jnp.where(lane_head((1, ROWS), HEAD) == h, 1.0, 0.0).astype(BF16) for h in range(4)]
             rows = slice(u * 4 * queries, (u + 1) * 4 * queries)
             seen[level][rows, :] = nt(jnp.concatenate(masked, 0), wk[:, part]).astype(BF16)
+            yield True
 
     def rows_of(level, whose):
         return half_of((h2, h3, h4)[level - 2], whose)[...]
@@ -376,48 +380,36 @@
 
     landed(hnear, 0, 192, recv01.at[0])
     project_side(hnear, 0)
-    units, near_lanes, base_near, one_near = side(0, 1 - core)
-    own_units = [base_own(h) for h in range(HEADS)]
-    run(own_units[:4])
-    halve_side(0)
-    run(own_units[4:] + units)
+    units, near_lanes, base_near = side(0, 1 - core)
+    mixed = [base_own(h) for h in range(HEADS)] + units
+    for place_in_line, level in ((9, 4), (6, 3), (3, 2)):
+        mixed.insert(place_in_line, look(level))
+    run(mixed)
     top, total, near_sums = by_head(base_near)
     merge(near_lanes, top, total, lambda h: near_sums[h])
-    for l in range(2, 5):
-        look(l)
 
     landed_or_zero(there[0], hfar, 0, 192, recv01.at[1])
-    h2[pl.ds(pl.multiple_of(mine(core), 64), 64), :] = nn(fold[...], hfar[...]).astype(BF16)
+    h2[pl.ds(pl.multiple_of(mine(core), 64), 64), :] = nn(fold[...], hfar[:192, :]).astype(BF16)
     landed_or_zero(there[1], h2, pl.multiple_of(mine(1 - core), 64), 64, recv_far.at[0])
     forward(h2, 0)
     finer(h2, odd, h3, 1 - odd)
-    project_side(hfar, 1)
     landed_or_zero(there[2], h3, pl.multiple_of(mine(1 - odd), 64), 64, recv_far.at[2])
     landed_or_zero(there[3], h3, pl.multiple_of(mine(odd) + odd * 32, 32), 32, recv_far.at[3])
     forward(h3, 1)
     finer(h3, second, h4, 1 - second)
-    halve_side(1)
+    project_side(hfar, 1)
     landed_or_zero(there[4], h4, pl.multiple_of(mine(1 - second), 64), 64, recv_far.at[4])
     landed_or_zero(there[5], h4, pl.multiple_of(mine(second) + second * 32, 32), 32, recv_far.at[5])
     forward(h4, 2)
 
-    units, far_lanes, base_far, one_far = side(1, core)
-    run(units)
-    missing = off(jnp.where(core == 0, me == 0, me == devices - 1))
+    missing = off(jnp.logical_not(there[0]))
+    units, far_lanes, base_far = side(1, core)
+    one = []
+    run(units + [level_one(j, missing, one) for j in range(HEADS // 2)])
     top, total, far_sums = by_head(base_far)
     merge(far_lanes, top - missing, total, lambda h: far_sums[h])
-    near_top, near_total, near_one = by_head(one_near)
-    far_top, far_total, far_one = by_head(one_far)
-    far_top = far_top - missing
-    top = jnp.maximum(near_top, far_top)
-    factor_near = jnp.exp2(near_top - top)
-    factor_far = jnp.exp2(far_top - top)
-    total = near_total * factor_near + far_total * factor_far
-    sums = [
-        (near_one[h] * factor_near[h : h + 1] + far_one[h] * factor_far[h : h + 1]).astype(BF16)
-        for h in range(HEADS)
-    ]
-    one_sums, top, total = spread_all(jnp.concatenate(sums, 0), top, total, spread1[...])
+    top, total, sums = by_head(one)
+    one_sums, top, total = spread_all(jnp.concatenate(sums, 0).astype(BF16), top, total, spread1[...])
     terms = [(top, total, lambda h: one_sums[head_rows(h)], 2.0)]
 
     vd[0] = values_of(core)
@@ -427,6 +419,11 @@
             scores[l, u] = nt(rows_of(l, core), seen[l][u * columns : (u + 1) * columns, :])
     for i, buffer in enumerate((h2, h3, h4)):
         landed(buffer, pl.multiple_of((1 - core) * BLOCK, BLOCK), BLOCK, recv_near.at[i])
+    loads[4].wait()
+    landed(deep, 0, 192 + 3 * BLOCK, send_sem.at[0])
+    for i, (here, rows) in enumerate(zip(there, (192, 64, 64, 32, 64, 32))):
+        pl.when(here)(lambda i=i, rows=rows: landed(deep, 0, rows, send_sem.at[i + 1]))
+
     vd[1] = values_of(1 - core)
     levels = [coarse(4, group, devices // 8), coarse(3, pair, devices // 4), coarse(2, chip, devices // 2)]
     run([unit for units, _ in levels for unit in units])
@@ -438,20 +435,16 @@
     lower = den[...] * factors[0]
     for factor, term in zip(factors[1:], terms):
         lower = lower + factor * term[1]
-    factors = [factor / lower for factor in factors]
+    inverse = 1.0 / lower
+    factors = [factor * inverse for factor in factors]
     attended = []
     for h in range(HEADS):
         upper = acc[head_rows(h), :] * factors[0][h : h + 1]
         for factor, term in zip(factors[1:], terms):
             upper = upper + term[2](h) * factor[h : h + 1]
         attended.append(upper.astype(BF16))
-    loads[4].wait()
     turned = nt(eye[...], jnp.concatenate(attended, 0)).astype(BF16)
     out_ref[...] = nn(turned, wo[...]).astype(BF16)
-
-    landed(deep, 0, 192 + 3 * BLOCK, send_sem.at[0])
-    for i, (here, rows) in enumerate(zip(there, (192, 64, 64, 32, 64, 32))):
-        pl.when(here)(lambda i=i, rows=rows: landed(deep, 0, rows, send_sem.at[i + 1]))
 
 
 def solution(mesh):
@@ -473,8 +466,8 @@
                 square,
                 square,
                 pltpu.VMEM((COARSE, WIDTH), BF16),
-                pltpu.VMEM((192, WIDTH), BF16),
-                pltpu.VMEM((192, WIDTH), BF16),
+                tall,
+                tall,
                 pltpu.VMEM((3 * ROWS, WIDTH), BF16),
                 tall,
                 pltpu.VMEM((COARSE, WIDTH), BF16),

time: 19.8 us -> 19.8 us (level)
  no operation moved by 1% of the time
where the time goes in v1:
time: 19.8 us; the launch traced here: 19.7 us
  Pallas kernels  19 us (96%)
  local copies, waits for them, and re-layouts  0.71 us (4%)
    pallas_call x1, Pallas kernels, local(): pl.pallas_call(functools.partial(kernel, devices), out_shape=jax.ShapeDty...  19 us
    unnamed x1, local copies, waits for them, and re-layouts  0.71 us

profile of v1, /device:TPU:256, one launch (start us, length us, event | category | flops | bytes accessed | tf_op | source)
XLA Modules:
  0.0 19.7 jit_solution(9427562507026970452)
XLA Ops:
  0.0 19.0 %hierarchical_attention.1 = bf16[256,512]{1,0:T(8,128)(2,1)S(1)} custom-call(bf16[256,512]{1,0:T(8,128)(2,1)} %x_hbm.1, bf16[512,512]{1,0:T(8,128)(2,1)} %wq_hbm.1, bf16[512,512]{1,0:T(8,128)(2,1)} %wk_hbm.1, bf16[512,512]{1,0:T(8,128)(2,1)} %wv_hbm.1, bf16[512,512]{1,0:T(8,128)(2,1)} %wo_hbm.1), custom_call_target="tpu_custom_call" | custom-call | tf_op jit(solution)/shard_map/hierarchical_attention/pallas_call | solution.py:456
  19.0 0.7 %copy.7 = bf16[256,512]{1,0:T(8,128)(2,1)} copy(bf16[256,512]{1,0:T(8,128)(2,1)S(1)} %hierarchical_attention.1) | data formatting | bytes 524288

commit v2 on v1

--- a/solution.py
+++ b/solution.py
@@ -117,9 +117,6 @@
     h2, h3, h4 = (deep.at[pl.ds(i * ROWS, ROWS)] for i in range(3))
     for l in range(1, 5):
         average[START[l] : START[l] + (ROWS >> l), :] = averager(ROWS >> l, ROWS, l)
-    loads[0].wait()
-    t[...] = nn(average[...], x[...]).astype(BF16)
-
     pl.semaphore_wait(barrier, expected)
 
     def send(source, target, landing, recv, sent):
@@ -141,6 +138,9 @@
 
     pl.when(there[0])(lambda: send_edge(beyond, core, hfar, recv01.at[1], 1))
     send_edge(twin, 1 - core, hnear, recv01.at[0], 0)
+
+    loads[0].wait()
+    t[...] = nn(average[...], x[...]).astype(BF16)
 
     def send_one_means(target, half, landing, recv, sent):
         means = pl.multiple_of((1 - half) * 64, 64)

time: 19.8 us -> 19.9 us (level)
  no operation moved by 1% of the time
where the time goes in v2:
time: 19.9 us; the launch traced here: 19.8 us
  Pallas kernels  19.1 us (96%)
  local copies, waits for them, and re-layouts  0.71 us (4%)
    pallas_call x1, Pallas kernels, local(): pl.pallas_call(functools.partial(kernel, devices), out_shape=jax.ShapeDty...  19.1 us
    unnamed x1, local copies, waits for them, and re-layouts  0.71 us

profile of v2, /device:TPU:256, one launch (start us, length us, event | category | flops | bytes accessed | tf_op | source)
XLA Modules:
  0.0 19.8 jit_solution(1845792580786993919)
XLA Ops:
  0.0 19.1 %hierarchical_attention.1 = bf16[256,512]{1,0:T(8,128)(2,1)S(1)} custom-call(bf16[256,512]{1,0:T(8,128)(2,1)} %x_hbm.1, bf16[512,512]{1,0:T(8,128)(2,1)} %wq_hbm.1, bf16[512,512]{1,0:T(8,128)(2,1)} %wk_hbm.1, bf16[512,512]{1,0:T(8,128)(2,1)} %wv_hbm.1, bf16[512,512]{1,0:T(8,128)(2,1)} %wo_hbm.1), custom_call_target="tpu_custom_call" | custom-call | tf_op jit(solution)/shard_map/hierarchical_attention/pallas_call | solution.py:456
  19.1 0.7 %copy.7 = bf16[256,512]{1,0:T(8,128)(2,1)} copy(bf16[256,512]{1,0:T(8,128)(2,1)S(1)} %hierarchical_attention.1) | data formatting | bytes 524288

commit v3 on v1

--- a/solution.py
+++ b/solution.py
@@ -107,7 +107,7 @@
         pl.semaphore_signal(barrier, inc=1, device_id=place(target), device_id_type=pl.DeviceIdType.MESH)
 
     expected = 1
-    for here, targets in zip(there, parties):
+    for here, targets in reversed(list(zip(there, parties))):
         expected = expected + jnp.where(here, len(targets), 0)
         pl.when(here)(lambda targets=targets: [signal(target) for target in targets] and None)
     signal(twin)
@@ -119,6 +119,23 @@
         average[START[l] : START[l] + (ROWS >> l), :] = averager(ROWS >> l, ROWS, l)
     loads[0].wait()
     t[...] = nn(average[...], x[...]).astype(BF16)
+
+    eye[...] = averager(ROWS, ROWS, 0)
+    halve[...] = averager(64, BLOCK, 1)
+    fold[:32, :] = jnp.concatenate([averager(32, BLOCK, 2), jnp.zeros((32, 64), BF16)], 1)
+    fold[32:, :] = jnp.concatenate([jnp.zeros((32, BLOCK), BF16), averager(32, 64, 1)], 1)
+    spreads = {1: spread1, 2: spread2, 3: spread3, 4: spread4}
+    for l in range(1, 5):
+        spreads[l][...] = spreader(spreads[l].shape[0], ROWS >> l, l)
+    for load in loads[1:4]:
+        load.wait()
+    q0[...] = (nn(x[...], wq[...]) * SCALE).astype(BF16)
+    k0[...] = nn(x[...], wk[...]).astype(BF16)
+    for i in range(2):
+        wvt[i * ROWS : (i + 1) * ROWS, :] = nt(eye[...], wv[:, i * ROWS : (i + 1) * ROWS]).astype(BF16)
+    ql[...] = nn(average[...], q0[...]).astype(BF16)
+    v0[...] = nt(wvt[...], x[...]).astype(BF16)
+
 
     pl.semaphore_wait(barrier, expected)
 
@@ -362,22 +379,6 @@
 
         return [unit(u) for u in range(HEADS // together)], gathered
 
-    eye[...] = averager(ROWS, ROWS, 0)
-    halve[...] = averager(64, BLOCK, 1)
-    fold[:32, :] = jnp.concatenate([averager(32, BLOCK, 2), jnp.zeros((32, 64), BF16)], 1)
-    fold[32:, :] = jnp.concatenate([jnp.zeros((32, BLOCK), BF16), averager(32, 64, 1)], 1)
-    spreads = {1: spread1, 2: spread2, 3: spread3, 4: spread4}
-    for l in range(1, 5):
-        spreads[l][...] = spreader(spreads[l].shape[0], ROWS >> l, l)
-    for load in loads[1:4]:
-        load.wait()
-    q0[...] = (nn(x[...], wq[...]) * SCALE).astype(BF16)
-    k0[...] = nn(x[...], wk[...]).astype(BF16)
-    for i in range(2):
-        wvt[i * ROWS : (i + 1) * ROWS, :] = nt(eye[...], wv[:, i * ROWS : (i + 1) * ROWS]).astype(BF16)
-    ql[...] = nn(average[...], q0[...]).astype(BF16)
-    v0[...] = nt(wvt[...], x[...]).astype(BF16)
-
     landed(hnear, 0, 192, recv01.at[0])
     project_side(hnear, 0)
     units, near_lanes, base_near = side(0, 1 - core)
@@ -390,6 +391,13 @@
 
     landed_or_zero(there[0], hfar, 0, 192, recv01.at[1])
     h2[pl.ds(pl.multiple_of(mine(core), 64), 64), :] = nn(fold[...], hfar[:192, :]).astype(BF16)
+    project_side(hfar, 1)
+    missing = off(jnp.logical_not(there[0]))
+    units, far_lanes, base_far = side(1, core)
+    run(units)
+    top, total, far_sums = by_head(base_far)
+    merge(far_lanes, top - missing, total, lambda h: far_sums[h])
+
     landed_or_zero(there[1], h2, pl.multiple_of(mine(1 - core), 64), 64, recv_far.at[0])
     forward(h2, 0)
     finer(h2, odd, h3, 1 - odd)
@@ -397,26 +405,20 @@
     landed_or_zero(there[3], h3, pl.multiple_of(mine(odd) + odd * 32, 32), 32, recv_far.at[3])
     forward(h3, 1)
     finer(h3, second, h4, 1 - second)
-    project_side(hfar, 1)
     landed_or_zero(there[4], h4, pl.multiple_of(mine(1 - second), 64), 64, recv_far.at[4])
     landed_or_zero(there[5], h4, pl.multiple_of(mine(second) + second * 32, 32), 32, recv_far.at[5])
     forward(h4, 2)
 
-    missing = off(jnp.logical_not(there[0]))
-    units, far_lanes, base_far = side(1, core)
     one = []
-    run(units + [level_one(j, missing, one) for j in range(HEADS // 2)])
-    top, total, far_sums = by_head(base_far)
-    merge(far_lanes, top - missing, total, lambda h: far_sums[h])
-    top, total, sums = by_head(one)
-    one_sums, top, total = spread_all(jnp.concatenate(sums, 0).astype(BF16), top, total, spread1[...])
-    terms = [(top, total, lambda h: one_sums[head_rows(h)], 2.0)]
-
+    run([level_one(j, missing, one) for j in range(HEADS // 2)])
     vd[0] = values_of(core)
     for l in range(4, 1, -1):
         _, together, columns = shape_of(l)
         for u in range(HEADS // together):
             scores[l, u] = nt(rows_of(l, core), seen[l][u * columns : (u + 1) * columns, :])
+    top, total, sums = by_head(one)
+    one_sums, top, total = spread_all(jnp.concatenate(sums, 0).astype(BF16), top, total, spread1[...])
+    terms = [(top, total, lambda h: one_sums[head_rows(h)], 2.0)]
     for i, buffer in enumerate((h2, h3, h4)):
         landed(buffer, pl.multiple_of((1 - core) * BLOCK, BLOCK), BLOCK, recv_near.at[i])
     loads[4].wait()

time: 19.8 us -> 19.9 us (level)
  the two profiles are of different devices: /device:TPU:256 before, /device:TPU:321 now
where the time goes in v3:
time: 19.9 us; the launch traced here: 19.8 us
  Pallas kernels  19.1 us (96%)
  local copies, waits for them, and re-layouts  0.71 us (4%)
    pallas_call x1, Pallas kernels, local(): pl.pallas_call(functools.partial(kernel, devices), out_shape=jax.ShapeDty...  19.1 us
    unnamed x1, local copies, waits for them, and re-layouts  0.71 us

profile of v3, /device:TPU:321, one launch (start us, length us, event | category | flops | bytes accessed | tf_op | source)
XLA Modules:
  0.0 19.8 jit_solution(9698443984001126081)
XLA Ops:
  0.0 19.1 %hierarchical_attention.1 = bf16[256,512]{1,0:T(8,128)(2,1)S(1)} custom-call(bf16[256,512]{1,0:T(8,128)(2,1)} %x_hbm.1, bf16[512,512]{1,0:T(8,128)(2,1)} %wq_hbm.1, bf16[512,512]{1,0:T(8,128)(2,1)} %wk_hbm.1, bf16[512,512]{1,0:T(8,128)(2,1)} %wv_hbm.1, bf16[512,512]{1,0:T(8,128)(2,1)} %wo_hbm.1), custom_call_target="tpu_custom_call" | custom-call | tf_op jit(solution)/shard_map/hierarchical_attention/pallas_call | solution.py:458
  19.1 0.7 %copy.7 = bf16[256,512]{1,0:T(8,128)(2,1)} copy(bf16[256,512]{1,0:T(8,128)(2,1)S(1)} %hierarchical_attention.1) | data formatting | bytes 524288
